TPU v7x, 256 devices: a whole 4x4x8 slice. The times are simulated.
256 devices in a mesh: ctx: 32 (over x, z), head: 8 (over y, core).
Axes of the slice: x: 4, y: 4, z: 8, core: 2. Of those that a mesh axis runs over, the one named last changes fastest.
Arguments:
- queries: bfloat16 [16384, 4096], P('ctx', 'head'), may hold values from -5 to 5
- key_rows: bfloat16 [16384, 1024], P('ctx', 'head'), may hold values from -5 to 5
- value_rows: bfloat16 [16384, 1024], P('ctx', 'head'), may hold values from -6 to 6
- slash_offsets: int32 [32, 4], P('head'), may hold values from 0 to 8, as said below
- union_blocks: int32 [8, 32, 2], P('head'), may hold values from 0 to 7, as said below
- head_picks: int32 [32, 32, 1], P('head'), may hold values from 0 to 1, as said below
- owner_counts: int32 [32, 32], P('head'), may hold values from 0 to 1, as said below
- out_weight: bfloat16 [4096, 4096], P(None, 'head'), may hold values from -0.09375 to 0.09375
Outputs:
- projected: bfloat16 [16384, 4096], P('ctx', 'head')
Inputs may be any that keep to these rules, and one draw needn't show every extreme that they name: `slash_offsets`: each head's offsets are distinct and include 0 and 8. `union_blocks`: the 2 entries of each KV head and sequence block are distinct. `head_picks`: the 1 entries of each query head and sequence block are distinct. `owner_counts`: equal to 1 for sequence block 0.
All inputs are finite; a program needn't handle non-finite values.
Results may differ from a plain program's by a relative error of at most 0.0056.
Values may be sent and summed in bfloat16 or wider, within the bound.
A program may use at most 128 MiB of HBM per device.

v0:
```python
import jax
import jax.numpy as jnp
from jax import lax
from jax.sharding import PartitionSpec as P

HEAD_SIZE = 128
BLOCK_TOKENS = 64
NS = 4
VPER = 1


def from_behind(array, axis, by):
    length = lax.axis_size(axis)
    pairs = [(i, i + by) for i in range(length) if 0 <= i + by < length]
    return lax.ppermute(array, axis, pairs)


def attend(
    vert_scores, vert_mask, diagonal_scores, slash_mask, vert_values, diagonal_values, per_dev
):
    masked_vert = jnp.where(vert_mask, vert_scores, -1e30)
    masked_slash = jnp.where(slash_mask, diagonal_scores, -1e30)
    peak = jnp.maximum(
        jnp.max(masked_vert, axis=-1, keepdims=True), jnp.max(masked_slash, axis=-1, keepdims=True)
    )
    weight_vert = jnp.exp(masked_vert - peak)
    weight_slash = jnp.exp(masked_slash - peak)
    total = jnp.sum(weight_vert, axis=-1, keepdims=True) + jnp.sum(
        weight_slash, axis=-1, keepdims=True
    )
    prob_vert = weight_vert.astype(jnp.bfloat16)
    slash_probability = weight_slash.astype(jnp.bfloat16).reshape(
        per_dev, BLOCK_TOKENS, NS, BLOCK_TOKENS
    )
    numer = jnp.dot(prob_vert, vert_values, preferred_element_type=jnp.float32)
    diagonal_portion = jnp.einsum(
        "wojf,wjfl->wol", slash_probability, diagonal_values, preferred_element_type=jnp.float32
    )
    numer = numer + diagonal_portion.reshape(per_dev * BLOCK_TOKENS, HEAD_SIZE)
    return (numer / total).astype(jnp.bfloat16)


def shards(
    queries, key_rows, value_rows, slash_offsets, union_blocks, head_picks, owner_counts, out_weight
):
    tokens = queries.shape[0]
    per_dev = tokens // BLOCK_TOKENS
    heads_here = slash_offsets.shape[0]
    groups_here = key_rows.shape[1] // HEAD_SIZE
    group_size = heads_here // groups_here
    owners = lax.axis_size("ctx")
    device_rank = lax.axis_index("ctx")
    scale_of_scores = jnp.float32(HEAD_SIZE ** (-0.5))
    stacked = jnp.stack([key_rows, value_rows])
    previous = from_behind(stacked, "ctx", 1)
    extended = jnp.concatenate([previous, stacked], axis=1).reshape(
        2, 2 * per_dev, BLOCK_TOKENS, groups_here, HEAD_SIZE
    )
    local_blocks = stacked.reshape(2, per_dev, BLOCK_TOKENS, groups_here, HEAD_SIZE)
    head_group = jnp.arange(heads_here, dtype=jnp.int32) // group_size
    mine_union = lax.dynamic_index_in_dim(union_blocks, device_rank, 1, keepdims=False)
    owner_base = jnp.arange(owners, dtype=jnp.int32)[:, None] * per_dev
    slot_rank = jnp.arange(VPER, dtype=jnp.int32)
    chosen = slot_rank[None, None, :] < owner_counts[:, :, None]
    mine_picks = lax.dynamic_index_in_dim(head_picks, device_rank, 1, keepdims=False)
    chosen_local = jnp.take_along_axis(mine_union[head_group], mine_picks, axis=1)
    block_rows = local_blocks[:, chosen_local, :, head_group[:, None], :]
    gathered = lax.all_gather(block_rows[:, None], "ctx", axis=1, tiled=True)
    slot_block = owner_base[None] + jnp.take_along_axis(
        union_blocks[head_group], head_picks, axis=2
    )
    source_of = list(range(heads_here))
    query_place = device_rank * tokens + jnp.arange(tokens, dtype=jnp.int32)
    query_block = device_rank * per_dev + jnp.arange(per_dev, dtype=jnp.int32)
    inner_offset = jnp.arange(BLOCK_TOKENS, dtype=jnp.int32)
    local_index = jnp.arange(per_dev, dtype=jnp.int32)
    per_head = []
    for head_index in range(heads_here):
        kv_index = head_index // group_size
        offsets = slash_offsets[head_index]
        query_head = queries[:, head_index * HEAD_SIZE : (head_index + 1) * HEAD_SIZE]
        vertical = gathered[source_of[head_index]]
        blocks_flat = slot_block[head_index].reshape(-1)
        valid_flat = chosen[head_index].reshape(-1)
        slot_count = blocks_flat.shape[0]
        vert_keys = vertical[:, :, 0].reshape(slot_count * BLOCK_TOKENS, HEAD_SIZE)
        vert_values = vertical[:, :, 1].reshape(slot_count * BLOCK_TOKENS, HEAD_SIZE)
        vert_scores = (
            jnp.einsum("qd,kd->qk", query_head, vert_keys, preferred_element_type=jnp.float32)
            * scale_of_scores
        )
        distance = query_block[:, None] - blocks_flat[None, :]
        on_slash = jnp.any(distance[:, :, None] == offsets[None, None, :], axis=2)
        block_mask = valid_flat[None, :] & jnp.logical_not(on_slash)
        key_place = (blocks_flat[:, None] * BLOCK_TOKENS + inner_offset[None, :]).reshape(-1)
        vert_mask = jnp.broadcast_to(
            block_mask[:, None, :, None], (per_dev, BLOCK_TOKENS, slot_count, BLOCK_TOKENS)
        ).reshape(tokens, slot_count * BLOCK_TOKENS)
        vert_mask = vert_mask & (key_place[None, :] <= query_place[:, None])
        group_slab = extended[:, :, :, kv_index, :]
        ext_index = local_index[:, None] + per_dev - offsets[None, :]
        slash_rows = group_slab[:, ext_index]
        diagonal_scores = (
            jnp.einsum(
                "hax,hisx->hais",
                query_head.reshape(per_dev, BLOCK_TOKENS, HEAD_SIZE),
                slash_rows[0],
                preferred_element_type=jnp.float32,
            )
            * scale_of_scores
        )
        slash_valid = query_block[:, None] - offsets[None, :] >= 0
        slash_mask = slash_valid[:, None, :, None] & (
            (offsets[None, None, :, None] > 0)
            | (inner_offset[None, None, None, :] <= inner_offset[None, :, None, None])
        )
        slash_mask = slash_mask.reshape(tokens, NS * BLOCK_TOKENS)
        per_head.append(
            attend(
                vert_scores,
                vert_mask,
                diagonal_scores.reshape(tokens, NS * BLOCK_TOKENS),
                slash_mask,
                vert_values,
                slash_rows[1],
                per_dev,
            )
        )
    attended = jnp.concatenate(per_head, axis=1)
    projected = jnp.dot(
        lax.all_gather(attended, "head", axis=1, tiled=True),
        out_weight,
        preferred_element_type=jnp.float32,
    )
    return projected.astype(jnp.bfloat16)


def solution(mesh):
    in_specs = (
        P("ctx", "head"),
        P("ctx", "head"),
        P("ctx", "head"),
        P("head", None),
        P("head", None, None),
        P("head", None, None),
        P("head", None),
        P(None, "head"),
    )
    out_specs = P("ctx", "head")
    return jax.shard_map(shards, mesh=mesh, in_specs=in_specs, out_specs=out_specs, check_vma=False)
```

profile of v0, /device:TPU:1, one launch (start us, length us, event | category | flops | bytes accessed | tf_op | source)
XLA Modules:
  0.0 189.1 jit_solution(1846127941252690670)
XLA Ops:
  6.5 0.8 constant_dynamic-slice_fusion
  7.5 0.9 dynamic-slice_reduce_fusion
  9.1 1.0 pad_maximum_fusion.1
  10.1 1.2 gather_fusion
  11.4 1.0 pad_maximum_fusion.2
  12.4 4.4 %collective-permute-start = (bf16[2,512,128]{2,1,0:T(8,128)(2,1)S(1)}, bf16[2,512,128]{2,1,0:T(8,128)(2,1)S(1)}, u32[]{:S(2)}, u32[]{:S(2)}) collective-permute-start(bf16[2,512,128]{2,1,0:T(8,128)(2,1)S(1)} %pad_maximum_fusion.2), channel_id=1, source_target_pairs={{0,8},{8,16},{16,24},{24,32},{32,40},{40,48},{48,56},{56,64},{64,7... | collective-permute-start | bytes 786440 | tf_op jit(solution)/shard_map/ppermute | solution.py:15
  16.8 0.7 fusion.89
  17.6 0.8 copy.55
  18.3 1.5 gather_fusion.5
  21.6 0.8 broadcast_or_fusion.3
  23.7 4.7 %reshape.1051 = pred[512,2048]{0,1:T(32,128)(4,1)} reshape(pred[8,64,32,64]{1,0,3,2:T(8,128)(4,1)S(1)} %broadcast_in_dim.29) | data formatting | bytes 2097152 | tf_op jit(solution)/shard_map/reshape | solution.py:98
  29.8 4.7 %reshape.1054 = pred[512,2048]{0,1:T(32,128)(4,1)} reshape(pred[8,64,32,64]{1,0,3,2:T(8,128)(4,1)S(1)} %broadcast_in_dim.33) | data formatting | bytes 2097152 | tf_op jit(solution)/shard_map/reshape | solution.py:98
  35.9 4.7 %reshape.1057 = pred[512,2048]{0,1:T(32,128)(4,1)} reshape(pred[8,64,32,64]{1,0,3,2:T(8,128)(4,1)S(1)} %broadcast_in_dim.34) | data formatting | bytes 2097152 | tf_op jit(solution)/shard_map/reshape | solution.py:98
  42.0 4.7 %reshape.1060 = pred[512,2048]{0,1:T(32,128)(4,1)} reshape(pred[8,64,32,64]{1,0,3,2:T(8,128)(4,1)S(1)} %broadcast_in_dim.35) | data formatting | bytes 2097152 | tf_op jit(solution)/shard_map/reshape | solution.py:98
  47.4 0.7 fusion.99
  48.2 0.7 gather_fusion.1
  49.1 1.0 copy-done.9
  50.0 1.3 fusion.107
  51.5 0.7 gather_fusion.2
  52.3 1.0 copy-done.8
  54.4 0.7 gather_fusion.3
  55.2 1.0 copy-done.7
  57.2 1.7 gather_fusion.4
  58.9 1.3 copy.70
  60.2 1.0 copy-done.5
  61.6 32.7 %all-gather.6.cloned.1.call-done = bf16[4,64,64,128]{3,2,1,0:T(8,128)(2,1)} async-done(((bf16[4,2,64,128]{3,2,1,0:T(8,128)(2,1)}), bf16[4,64,64,128]{3,2,1,0:T(8,128)(2,1)}) %all-gather.6.cloned.1.call-update) | async-done | bytes 4194320 | tf_op jit(solution)/shard_map/all_gather | solution.py:68
  94.4 4.4 %fusion.94 = (bf16[1,64,64,128]{3,2,1,0:T(8,128)(2,1)S(1)}, bf16[1,64,64,128]{3,2,1,0:T(8,128)(2,1)}, bf16[1,64,64,128]{3,2,1,0:T(8,128)(2,1)}, bf16[1,64,64,128]{3,2,1,0:T(8,128)(2,1)}) fusion(bf16[4,64,64,128]{3,2,1,0:T(8,128)(2,1)} %all-gather.6.cloned.1.call-done), kind=kLoop, calls=%fused_computation.176 | loop fusion | bytes 8388608 | tf_op jit(solution)/shard_map/slice | solution.py:82
  98.7 0.9 fusion.95
  99.6 3.6 %fusion.106 = (f32[512]{0:T(512)S(1)}, f32[512,2048]{0,1:T(8,128)}) fusion(bf16[2048,128]{1,0:T(8,128)(2,1)S(1)} %bitcast.252, bf16[512,512]{1,0:T(8,128)(2,1)} %param.8, pred[512,2048]{0,1:T(32,128)(4,1)S(1)} %copy-done.19, s32[512]{0:T(512)S(1)} %copy-done.37, s32[2048]{0:T(1024)S(1)} %copy-done.32), kind=kOutput, calls=%fused_computation.188 | convolution fusion | flops 273677824 | bytes 5910528 | tf_op jit(solution)/shard_map/qd,kd->qk/dot_general | solution.py:89
  103.3 1.5 fusion.64
  104.8 1.7 fusion.78
  106.5 2.1 %fusion.96 = (bf16[32,1,1,64,128]{4,3,2,0,1:T(8,128)(2,1)}, bf16[32,1,1,64,128]{4,3,2,0,1:T(8,128)(2,1)S(1)}) fusion(bf16[32,1,2,64,128]{4,3,2,0,1:T(8,128)(2,1)} %bitcast.227), kind=kLoop, calls=%fused_computation.178 | loop fusion | bytes 2097152 | tf_op jit(solution)/shard_map/slice | solution.py:87
  108.6 3.6 %fusion.104 = (f32[512]{0:T(512)S(1)}, f32[512,2048]{0,1:T(8,128)}) fusion(bf16[2048,128]{1,0:T(8,128)(2,1)S(1)} %bitcast.253, bf16[512,512]{1,0:T(8,128)(2,1)} %param.8, pred[512,2048]{0,1:T(32,128)(4,1)S(1)} %copy-done.18, s32[512]{0:T(512)S(1)} %copy-done.37, s32[2048]{0:T(1024)S(1)} %copy-done.31), kind=kOutput, calls=%fused_computation.186 | convolution fusion | flops 273677824 | bytes 5910528 | tf_op jit(solution)/shard_map/qd,kd->qk/dot_general | solution.py:89
  112.5 2.2 %fusion.76 = f32[8,64,128,1]{2,1,3,0:T(8,128)} fusion(f32[8,64,4,64]{1,3,2,0:T(8,128)S(1)} %get-tuple-element.68, bf16[2,8,4,64,128]{4,3,2,1,0:T(8,128)(2,1)} %bitcast.234, f32[8,64]{1,0:T(8,128)S(1)} %max.47), kind=kOutput, calls=%fused_computation.70 | convolution fusion | flops 33816576 | bytes 1312768 | tf_op jit(solution)/shard_map/wojf,wjfl->wol/dot_general | solution.py:36
  114.7 2.1 %fusion.97 = (bf16[32,1,1,64,128]{4,3,2,0,1:T(8,128)(2,1)}, bf16[32,1,1,64,128]{4,3,2,0,1:T(8,128)(2,1)S(1)}) fusion(bf16[32,1,2,64,128]{4,3,2,0,1:T(8,128)(2,1)} %bitcast.226), kind=kLoop, calls=%fused_computation.179 | loop fusion | bytes 2097152 | tf_op jit(solution)/shard_map/slice | solution.py:87
  116.8 3.7 %fusion.102 = (f32[512]{0:T(512)S(1)}, f32[512,2048]{0,1:T(8,128)}) fusion(bf16[2048,128]{1,0:T(8,128)(2,1)S(1)} %bitcast.254, bf16[512,512]{1,0:T(8,128)(2,1)} %param.8, pred[512,2048]{0,1:T(32,128)(4,1)S(1)} %copy-done.17, s32[512]{0:T(512)S(1)} %copy-done.37, s32[2048]{0:T(1024)S(1)} %copy-done.30), kind=kOutput, calls=%fused_computation.184 | convolution fusion | flops 273677824 | bytes 5910528 | tf_op jit(solution)/shard_map/qd,kd->qk/dot_general | solution.py:89
  120.8 2.2 %fusion.74 = f32[8,64,128,1]{2,1,3,0:T(8,128)} fusion(f32[8,64,4,64]{1,3,2,0:T(8,128)S(1)} %get-tuple-element.64, bf16[2,8,4,64,128]{4,3,2,1,0:T(8,128)(2,1)} %bitcast.232, f32[8,64]{1,0:T(8,128)S(1)} %max.49), kind=kOutput, calls=%fused_computation.69 | convolution fusion | flops 33816576 | bytes 1312768 | tf_op jit(solution)/shard_map/wojf,wjfl->wol/dot_general | solution.py:36
  122.9 0.9 fusion.98
  123.9 3.7 %fusion.100 = (f32[512]{0:T(512)S(1)}, f32[512,2048]{0,1:T(8,128)}) fusion(bf16[2048,128]{1,0:T(8,128)(2,1)S(1)} %bitcast.251, bf16[512,512]{1,0:T(8,128)(2,1)} %param.8, pred[512,2048]{0,1:T(32,128)(4,1)S(1)} %copy-done.16, s32[512]{0:T(512)S(1)} %copy-done.37, s32[2048]{0:T(1024)S(1)} %copy-done.29), kind=kOutput, calls=%fused_computation.182 | convolution fusion | flops 273677824 | bytes 5910528 | tf_op jit(solution)/shard_map/qd,kd->qk/dot_general | solution.py:89
  129.1 3.0 %fusion = f32[512]{0:T(512)S(1)} fusion(f32[512,2048]{0,1:T(8,128)} %get-tuple-element.70, f32[512]{0:T(512)S(1)} %max.44), kind=kLoop, calls=%fused_computation.15 | loop fusion | flops 2096640 | bytes 4198400 | tf_op jit(solution)/shard_map/reduce_sum | solution.py:28
  134.5 0.8 copy-done.3
  136.5 0.8 fusion.61
  137.3 0.7 fusion.58
  138.1 0.8 fusion.55
  138.8 0.8 fusion.52
  139.6 0.8 pad_maximum_fusion
  140.5 35.2 %all-gather.4.cloned.1.call-done = bf16[512,4096]{0,1:T(8,128)(2,1)} async-done(((bf16[512,512]{0,1:T(8,128)(2,1)}), bf16[512,4096]{0,1:T(8,128)(2,1)}) %all-gather.4.cloned.1.call-update) | async-done | bytes 4194320 | tf_op jit(solution)/shard_map/all_gather | solution.py:131
  175.7 6.6 %convolution_convert_fusion = bf16[512,512]{1,0:T(8,128)(2,1)} fusion(bf16[512,4096]{0,1:T(8,128)(2,1)} %all-gather.4.cloned.1.call-done, bf16[4096,512]{1,0:T(8,128)(2,1)} %param.15), kind=kOutput, calls=%fused_computation.43 | convolution fusion | flops 2147745792 | bytes 8912896 | tf_op jit(solution)/shard_map/dot_general | solution.py:130
  (186 shorter events, 17.3 us)
Async XLA Ops:
  6.5 13.9 %copy-start.28 = (s32[4,32,1]{1,2,0:T(1,128)S(1)}, s32[4,32,1]{1,2,0:T(1,128)}, u32[]{:S(2)}) copy-start(s32[4,32,1]{1,2,0:T(1,128)} %param.13) | copy-start | bytes 1540
  6.5 13.4 %copy-start.35 = (s32[4,4]{1,0:T(4,128)S(1)}, s32[4,4]{1,0:T(4,128)}, u32[]{:S(2)}) copy-start(s32[4,4]{1,0:T(4,128)} %param.11) | copy-start | bytes 196
  6.5 14.2 %copy-start.36 = (s32[4,32]{1,0:T(4,128)S(1)}, s32[4,32]{1,0:T(4,128)}, u32[]{:S(2)}) copy-start(s32[4,32]{1,0:T(4,128)} %param.14) | copy-start | bytes 1540
  6.5 87.8 %all-gather.6.cloned.1.call-start = ((), (), s32[]{:S(2)}) async-start(), calls=%async_computation.1 | async-start | bytes 4325376 | tf_op jit(solution)/shard_map/all_gather | solution.py:68
  11.3 164.4 %all-gather.4.cloned.1.call-start = ((), (), s32[]{:S(2)}) async-start(), calls=%async_computation | async-start | bytes 4718592 | tf_op jit(solution)/shard_map/all_gather | solution.py:131
  12.4 35.8 %collective-permute-start = (bf16[2,512,128]{2,1,0:T(8,128)(2,1)S(1)}, bf16[2,512,128]{2,1,0:T(8,128)(2,1)S(1)}, u32[]{:S(2)}, u32[]{:S(2)}) collective-permute-start(bf16[2,512,128]{2,1,0:T(8,128)(2,1)S(1)} %pad_maximum_fusion.2), channel_id=1, source_target_pairs={{0,8},{8,16},{16,24},{24,32},{32,40},{40,48},{48,56},{56,64},{64,7... | collective-permute-start | bytes 786440 | tf_op jit(solution)/shard_map/ppermute | solution.py:15
  35.9 11.5 %copy-start.22 = (bf16[512,512]{1,0:T(8,128)(2,1)S(1)}, bf16[512,512]{1,0:T(8,128)(2,1)}, u32[]{:S(2)}) copy-start(bf16[512,512]{1,0:T(8,128)(2,1)} %param.8) | copy-start | bytes 1572868
  35.9 12.2 %copy-start.14 = (bf16[512,128]{1,0:T(8,128)(2,1)S(1)}, bf16[512,128]{1,0:T(8,128)(2,1)}, u32[]{:S(2)}) copy-start(bf16[512,128]{1,0:T(8,128)(2,1)} %param.10) | copy-start | bytes 393220
  35.9 12.2 %copy-start.15 = (bf16[512,128]{1,0:T(8,128)(2,1)S(1)}, bf16[512,128]{1,0:T(8,128)(2,1)}, u32[]{:S(2)}) copy-start(bf16[512,128]{1,0:T(8,128)(2,1)} %param.9) | copy-start | bytes 393220
  46.7 3.3 %copy-start.27 = (pred[64,4,64]{0,2,1:T(8,128)(4,1)S(1)}, pred[64,4,64]{0,2,1:T(8,128)(4,1)}, u32[]{:S(2)}) copy-start(pred[64,4,64]{0,2,1:T(8,128)(4,1)} %get-tuple-element.21) | copy-start | bytes 49156
  46.7 3.3 %copy-start.41 = (pred[8,4]{1,0:T(8,128)(4,1)S(1)}, pred[8,4]{1,0:T(8,128)(4,1)}, u32[]{:S(2)}) copy-start(pred[8,4]{1,0:T(8,128)(4,1)} %get-tuple-element.49) | copy-start | bytes 100
  49.0 4.4 %copy-start.26 = (pred[64,4,64]{0,2,1:T(8,128)(4,1)S(1)}, pred[64,4,64]{0,2,1:T(8,128)(4,1)}, u32[]{:S(2)}) copy-start(pred[64,4,64]{0,2,1:T(8,128)(4,1)} %get-tuple-element.22) | copy-start | bytes 49156
  49.0 4.4 %copy-start.40 = (pred[8,4]{1,0:T(8,128)(4,1)S(1)}, pred[8,4]{1,0:T(8,128)(4,1)}, u32[]{:S(2)}) copy-start(pred[8,4]{1,0:T(8,128)(4,1)} %get-tuple-element.50) | copy-start | bytes 100
  49.1 1.0 copy-start.9
  52.2 4.0 %copy-start.23 = (bf16[512,128]{1,0:T(8,128)(2,1)S(1)}, bf16[512,128]{1,0:T(8,128)(2,1)}, u32[]{:S(2)}) copy-start(bf16[512,128]{1,0:T(8,128)(2,1)} %get-tuple-element.20) | copy-start | bytes 393220
  52.2 4.0 %copy-start.25 = (pred[64,4,64]{0,2,1:T(8,128)(4,1)S(1)}, pred[64,4,64]{0,2,1:T(8,128)(4,1)}, u32[]{:S(2)}) copy-start(pred[64,4,64]{0,2,1:T(8,128)(4,1)} %get-tuple-element.23) | copy-start | bytes 49156
  52.2 4.0 %copy-start.39 = (pred[8,4]{1,0:T(8,128)(4,1)S(1)}, pred[8,4]{1,0:T(8,128)(4,1)}, u32[]{:S(2)}) copy-start(pred[8,4]{1,0:T(8,128)(4,1)} %get-tuple-element.51) | copy-start | bytes 100
  52.3 1.0 copy-start.8
  55.1 6.1 %copy-start.24 = (pred[64,4,64]{0,2,1:T(8,128)(4,1)S(1)}, pred[64,4,64]{0,2,1:T(8,128)(4,1)}, u32[]{:S(2)}) copy-start(pred[64,4,64]{0,2,1:T(8,128)(4,1)} %get-tuple-element.24) | copy-start | bytes 49156
  55.1 6.1 %copy-start.38 = (pred[8,4]{1,0:T(8,128)(4,1)S(1)}, pred[8,4]{1,0:T(8,128)(4,1)}, u32[]{:S(2)}) copy-start(pred[8,4]{1,0:T(8,128)(4,1)} %get-tuple-element.52) | copy-start | bytes 100
  55.2 1.0 copy-start.7
  60.2 1.0 copy-start.5
  61.6 38.0 %copy-start.32 = (s32[2048]{0:T(1024)S(1)}, s32[2048]{0:T(1024)}, u32[]{:S(2)}) copy-start(s32[2048]{0:T(1024)} %add.293) | copy-start | bytes 24580
  61.6 38.0 %copy-start.37 = (s32[512]{0:T(512)S(1)}, s32[512]{0:T(512)}, u32[]{:S(2)}) copy-start(s32[512]{0:T(512)} %iota_add_fusion.4) | copy-start | bytes 6148
  94.4 5.3 %copy-start.19 = (pred[512,2048]{0,1:T(32,128)(4,1)S(1)}, pred[512,2048]{0,1:T(32,128)(4,1)}, u32[]{:S(2)}) copy-start(pred[512,2048]{0,1:T(32,128)(4,1)} %reshape.1051) | copy-start | bytes 3145732
  99.6 8.9 %copy-start.31 = (s32[2048]{0:T(1024)S(1)}, s32[2048]{0:T(1024)}, u32[]{:S(2)}) copy-start(s32[2048]{0:T(1024)} %add.307) | copy-start | bytes 24580
  103.3 5.3 %copy-start.18 = (pred[512,2048]{0,1:T(32,128)(4,1)S(1)}, pred[512,2048]{0,1:T(32,128)(4,1)}, u32[]{:S(2)}) copy-start(pred[512,2048]{0,1:T(32,128)(4,1)} %reshape.1054) | copy-start | bytes 3145732
  108.6 8.2 %copy-start.30 = (s32[2048]{0:T(1024)S(1)}, s32[2048]{0:T(1024)}, u32[]{:S(2)}) copy-start(s32[2048]{0:T(1024)} %add.314) | copy-start | bytes 24580
  112.3 4.5 %copy-start.17 = (pred[512,2048]{0,1:T(32,128)(4,1)S(1)}, pred[512,2048]{0,1:T(32,128)(4,1)}, u32[]{:S(2)}) copy-start(pred[512,2048]{0,1:T(32,128)(4,1)} %reshape.1057) | copy-start | bytes 3145732
  116.8 6.2 %copy-start.4 = (bf16[1,64,64,128]{3,2,1,0:T(8,128)(2,1)S(1)}, bf16[1,64,64,128]{3,2,1,0:T(8,128)(2,1)}, u32[]{:S(2)}) copy-start(bf16[1,64,64,128]{3,2,1,0:T(8,128)(2,1)} %get-tuple-element.8) | copy-start | bytes 3145732
  116.8 7.0 %copy-start.29 = (s32[2048]{0:T(1024)S(1)}, s32[2048]{0:T(1024)}, u32[]{:S(2)}) copy-start(s32[2048]{0:T(1024)} %add.321) | copy-start | bytes 24580
  120.6 3.3 %copy-start.16 = (pred[512,2048]{0,1:T(32,128)(4,1)S(1)}, pred[512,2048]{0,1:T(32,128)(4,1)}, u32[]{:S(2)}) copy-start(pred[512,2048]{0,1:T(32,128)(4,1)} %reshape.1060) | copy-start | bytes 3145732
  123.8 4.0 %copy-start.6 = (bf16[32,2,64,128]{3,2,0,1:T(8,128)(2,1)S(1)}, bf16[32,2,64,128]{3,2,0,1:T(8,128)(2,1)}, u32[]{:S(2)}) copy-start(bf16[32,2,64,128]{3,2,0,1:T(8,128)(2,1)} %copy-done.5) | copy-start | bytes 3145732
  123.8 4.6 %copy-start.33 = (f32[512]{0:T(512)S(1)}, f32[512]{0:T(512)}, u32[]{:S(2)}) copy-start(f32[512]{0:T(512)} %reduce_max.94) | copy-start | bytes 6148
  123.8 4.7 %copy-start.20 = (f32[8,64,128,1]{2,1,3,0:T(8,128)S(1)}, f32[8,64,128,1]{2,1,3,0:T(8,128)}, u32[]{:S(2)}) copy-start(f32[8,64,128,1]{2,1,3,0:T(8,128)} %fusion.76) | copy-start | bytes 786436
  123.8 4.8 %copy-start.34 = (f32[512]{0:T(512)S(1)}, f32[512]{0:T(512)}, u32[]{:S(2)}) copy-start(f32[512]{0:T(512)} %reduce_max.98) | copy-start | bytes 6148
  123.9 4.9 %copy-start.21 = (f32[8,64,128,1]{2,1,3,0:T(8,128)S(1)}, f32[8,64,128,1]{2,1,3,0:T(8,128)}, u32[]{:S(2)}) copy-start(f32[8,64,128,1]{2,1,3,0:T(8,128)} %fusion.74) | copy-start | bytes 786436
  128.9 6.9 %copy-start.10 = (bf16[32,1,1,64,128]{4,3,2,0,1:T(8,128)(2,1)S(1)}, bf16[32,1,1,64,128]{4,3,2,0,1:T(8,128)(2,1)}, u32[]{:S(2)}) copy-start(bf16[32,1,1,64,128]{4,3,2,0,1:T(8,128)(2,1)} %get-tuple-element.9) | copy-start | bytes 1572868
  129.1 3.5 %copy-start.1 = (f32[512,2048]{0,1:T(8,128)S(1)}, f32[512,2048]{0,1:T(8,128)}, u32[]{:S(2)}) copy-start(f32[512,2048]{0,1:T(8,128)} %get-tuple-element.66) | copy-start | bytes 12582916
  129.1 4.7 %copy-start.2 = (f32[512,2048]{0,1:T(8,128)S(1)}, f32[512,2048]{0,1:T(8,128)}, u32[]{:S(2)}) copy-start(f32[512,2048]{0,1:T(8,128)} %get-tuple-element.62) | copy-start | bytes 12582916
  132.6 2.7 %copy-start.3 = (f32[512,2048]{0,1:T(8,128)S(1)}, f32[512,2048]{0,1:T(8,128)}, u32[]{:S(2)}) copy-start(f32[512,2048]{0,1:T(8,128)} %get-tuple-element.58) | copy-start | bytes 12582916
  133.8 2.7 %copy-start = (f32[512,2048]{0,1:T(8,128)S(1)}, f32[512,2048]{0,1:T(8,128)}, u32[]{:S(2)}) copy-start(f32[512,2048]{0,1:T(8,128)} %get-tuple-element.70) | copy-start | bytes 12582916
  135.3 2.0 %copy-start.11 = (bf16[32,1,1,64,128]{4,3,2,0,1:T(8,128)(2,1)S(1)}, bf16[32,1,1,64,128]{4,3,2,0,1:T(8,128)(2,1)}, u32[]{:S(2)}) copy-start(bf16[32,1,1,64,128]{4,3,2,0,1:T(8,128)(2,1)} %get-tuple-element.11) | copy-start | bytes 1572868
  136.5 1.5 copy-start.12
  137.3 1.5 copy-start.13
Sparse Core Ops, SparseCore 0:
  11.4 82.9 all-gather.5
  140.6 35.0 all-gather.3
where the time goes:
time: 190 us; the launch traced here: 189 us
  waiting for transfers between devices  68 us (36%)
  local copies, waits for them, and re-layouts  56.4 us (30%)
  matrix products  33.1 us (17%)
  between operations  14.1 us (7%)
  other arithmetic  13.2 us (7%)
  starting transfers between devices  4.43 us (2%)
    all_gather x1, waiting for transfers between devices, shards(): lax.all_gather(attended, 'head', axis=1, tiled=True)  35.2 us
    all_gather x1, waiting for transfers between devices, shards(): gathered = lax.all_gather(block_rows[:, None], 'ctx', axis=1, tiled=True)  32.7 us
    reshape x4, local copies, waits for them, and re-layouts, shards(): vert_mask = jnp.broadcast_to(block_mask[:, None, :, None], (per_dev, BLOC...  18.9 us
    dot_general x4, matrix products, shards(): jnp.einsum('qd,kd->qk', query_head, vert_keys, preferred_element_type=jnp...  14.6 us
    unnamed x88, local copies, waits for them, and re-layouts  6.68 us
    dot_general x1, matrix products, shards(): jnp.dot(lax.all_gather(attended, 'head', axis=1, tiled=True), out_weight,...  6.61 us
    dot_general x4, matrix products, attend(): jnp.einsum('wojf,wjfl->wol', slash_probability, diagonal_values, preferre...  6.35 us
    slice x4, local copies, waits for them, and re-layouts, shards(): vertical[:, :, 1].reshape(slot_count * BLOCK_TOKENS, HEAD_SIZE)  5.9 us
  transfers between devices with their start and end apart: 3, of which 2 were waited for; matrix products, arithmetic and copies ran while one was open for 22% of the time, Pallas kernels for 0%

commit v1 on v0

--- a/solution.py
+++ b/solution.py
@@ -7,6 +7,14 @@
 BLOCK_TOKENS = 64
 NS = 4
 VPER = 1
+
+
+def gather_by_exchange(array, axis, dim):
+    size = lax.axis_size(axis)
+    repeats = [size if d == dim else 1 for d in range(array.ndim)]
+    return lax.all_to_all(
+        jnp.tile(array, repeats), axis, split_axis=dim, concat_axis=dim, tiled=True
+    )
 
 
 def from_behind(array, axis, by):
@@ -128,9 +136,7 @@
         )
     attended = jnp.concatenate(per_head, axis=1)
     projected = jnp.dot(
-        lax.all_gather(attended, "head", axis=1, tiled=True),
-        out_weight,
-        preferred_element_type=jnp.float32,
+        gather_by_exchange(attended, "head", 1), out_weight, preferred_element_type=jnp.float32
     )
     return projected.astype(jnp.bfloat16)
 

time: 190 us -> 218 us (1.15)
  blocking collectives: 0 us -> 56.8 us
  waiting for transfers between devices: 68 us -> 32.8 us
  local copies, waits for them, and re-layouts: 56.4 us -> 63.4 us
    all_to_all x0 -> x1, blocking collectives: none -> 56.8 us  [gather_by_exchange(): lax.all_to_all(jnp.tile(array, repeats), axis, split_axis=dim, concat_axi...]
    all_gather x1 -> x0, waiting for transfers between devices: 35.2 us -> none  [shards(): lax.all_gather(attended, 'head', axis=1, tiled=True)]
    all_to_all x0 -> x1, local copies, waits for them, and re-layouts: none -> 6.51 us  [gather_by_exchange(): lax.all_to_all(jnp.tile(array, repeats), axis, split_axis=dim, concat_axi...]
  transfers between devices with their start and end apart: 3 -> 2, of which waited for: 2 -> 1; matrix products, arithmetic and copies ran while one was open for 22% -> 19% of each run, Pallas kernels for 0% -> 0%
where the time goes in v1:
time: 218 us; the launch traced here: 217 us
  local copies, waits for them, and re-layouts  63.4 us (29%)
  blocking collectives  56.8 us (26%)
  matrix products  33 us (15%)
  waiting for transfers between devices  32.8 us (15%)
  between operations  14.1 us (6%)
  other arithmetic  12.4 us (6%)
  starting transfers between devices  4.39 us (2%)
    all_to_all x1, blocking collectives, gather_by_exchange(): lax.all_to_all(jnp.tile(array, repeats), axis, split_axis=dim, concat_axi...  56.8 us
    all_gather x1, waiting for transfers between devices, shards(): gathered = lax.all_gather(block_rows[:, None], 'ctx', axis=1, tiled=True)  32.8 us
    reshape x4, local copies, waits for them, and re-layouts, shards(): vert_mask = jnp.broadcast_to(block_mask[:, None, :, None], (per_dev, BLOC...  18.8 us
    dot_general x4, matrix products, shards(): jnp.einsum('qd,kd->qk', query_head, vert_keys, preferred_element_type=jnp...  14.6 us
    unnamed x88, local copies, waits for them, and re-layouts  6.65 us
    dot_general x1, matrix products, shards(): jnp.dot(gather_by_exchange(attended, 'head', 1), out_weight, preferred_el...  6.61 us
    all_to_all x1, local copies, waits for them, and re-layouts, gather_by_exchange(): lax.all_to_all(jnp.tile(array, repeats), axis, split_axis=dim, concat_axi...  6.51 us
    dot_general x4, matrix products, attend(): jnp.einsum('wojf,wjfl->wol', slash_probability, diagonal_values, preferre...  6.32 us
  transfers between devices with their start and end apart: 2, of which 1 were waited for; matrix products, arithmetic and copies ran while one was open for 19% of the time, Pallas kernels for 0%

profile of v1, /device:TPU:1, one launch (start us, length us, event | category | flops | bytes accessed | tf_op | source)
XLA Modules:
  0.0 216.9 jit_solution(16728484728419785104)
XLA Ops:
  6.5 0.8 constant_dynamic-slice_fusion
  7.5 0.9 dynamic-slice_reduce_fusion
  9.1 1.0 pad_maximum_fusion.1
  10.1 1.2 gather_fusion
  11.3 1.0 pad_maximum_fusion.2
  12.3 4.4 %collective-permute-start = (bf16[2,512,128]{2,1,0:T(8,128)(2,1)S(1)}, bf16[2,512,128]{2,1,0:T(8,128)(2,1)S(1)}, u32[]{:S(2)}, u32[]{:S(2)}) collective-permute-start(bf16[2,512,128]{2,1,0:T(8,128)(2,1)S(1)} %pad_maximum_fusion.2), channel_id=1, source_target_pairs={{0,8},{8,16},{16,24},{24,32},{32,40},{40,48},{48,56},{56,64},{64,7... | collective-permute-start | bytes 786440 | tf_op jit(solution)/shard_map/ppermute | solution.py:23
  16.7 0.7 fusion.89
  17.5 0.8 copy.81
  18.3 1.5 gather_fusion.5
  21.6 0.8 broadcast_or_fusion.3
  23.6 4.7 %reshape.1058 = pred[512,2048]{0,1:T(32,128)(4,1)} reshape(pred[8,64,32,64]{1,0,3,2:T(8,128)(4,1)S(1)} %broadcast_in_dim.29) | data formatting | bytes 2097152 | tf_op jit(solution)/shard_map/reshape | solution.py:106
  29.7 4.7 %reshape.1061 = pred[512,2048]{0,1:T(32,128)(4,1)} reshape(pred[8,64,32,64]{1,0,3,2:T(8,128)(4,1)S(1)} %broadcast_in_dim.33) | data formatting | bytes 2097152 | tf_op jit(solution)/shard_map/reshape | solution.py:106
  35.8 4.7 %reshape.1064 = pred[512,2048]{0,1:T(32,128)(4,1)} reshape(pred[8,64,32,64]{1,0,3,2:T(8,128)(4,1)S(1)} %broadcast_in_dim.34) | data formatting | bytes 2097152 | tf_op jit(solution)/shard_map/reshape | solution.py:106
  41.9 4.7 %reshape.1067 = pred[512,2048]{0,1:T(32,128)(4,1)} reshape(pred[8,64,32,64]{1,0,3,2:T(8,128)(4,1)S(1)} %broadcast_in_dim.35) | data formatting | bytes 2097152 | tf_op jit(solution)/shard_map/reshape | solution.py:106
  47.3 0.7 fusion.99
  48.1 0.7 gather_fusion.1
  49.0 1.0 copy-done.9
  49.9 1.3 fusion.107
  51.3 0.7 gather_fusion.2
  52.2 1.0 copy-done.8
  54.2 0.7 gather_fusion.3
  55.1 1.0 copy-done.7
  57.1 1.6 gather_fusion.4
  58.8 1.3 copy.96
  60.1 1.0 copy-done.5
  61.5 32.8 %all-gather.3.cloned.1.call-done = bf16[4,64,64,128]{3,2,1,0:T(8,128)(2,1)} async-done(((bf16[4,2,64,128]{3,2,1,0:T(8,128)(2,1)}), bf16[4,64,64,128]{3,2,1,0:T(8,128)(2,1)}) %all-gather.3.cloned.1.call-update) | async-done | bytes 4194320 | tf_op jit(solution)/shard_map/all_gather | solution.py:76
  94.3 4.4 %fusion.94 = (bf16[1,64,64,128]{3,2,1,0:T(8,128)(2,1)S(1)}, bf16[1,64,64,128]{3,2,1,0:T(8,128)(2,1)}, bf16[1,64,64,128]{3,2,1,0:T(8,128)(2,1)}, bf16[1,64,64,128]{3,2,1,0:T(8,128)(2,1)}) fusion(bf16[4,64,64,128]{3,2,1,0:T(8,128)(2,1)} %all-gather.3.cloned.1.call-done), kind=kLoop, calls=%fused_computation.176 | loop fusion | bytes 8388608 | tf_op jit(solution)/shard_map/slice | solution.py:90
  98.7 0.9 fusion.95
  99.6 3.6 %fusion.106 = (f32[512]{0:T(512)S(1)}, f32[512,2048]{0,1:T(8,128)}) fusion(bf16[2048,128]{1,0:T(8,128)(2,1)S(1)} %bitcast.254, bf16[512,512]{1,0:T(8,128)(2,1)} %param.8, pred[512,2048]{0,1:T(32,128)(4,1)S(1)} %copy-done.19, s32[512]{0:T(512)S(1)} %copy-done.37, s32[2048]{0:T(1024)S(1)} %copy-done.32), kind=kOutput, calls=%fused_computation.188 | convolution fusion | flops 273677824 | bytes 5910528 | tf_op jit(solution)/shard_map/qd,kd->qk/dot_general | solution.py:97
  103.3 1.5 fusion.64
  104.8 1.7 fusion.78
  106.5 2.1 fusion.96
  108.6 3.6 %fusion.104 = (f32[512]{0:T(512)S(1)}, f32[512,2048]{0,1:T(8,128)}) fusion(bf16[2048,128]{1,0:T(8,128)(2,1)S(1)} %bitcast.255, bf16[512,512]{1,0:T(8,128)(2,1)} %param.8, pred[512,2048]{0,1:T(32,128)(4,1)S(1)} %copy-done.18, s32[512]{0:T(512)S(1)} %copy-done.37, s32[2048]{0:T(1024)S(1)} %copy-done.31), kind=kOutput, calls=%fused_computation.186 | convolution fusion | flops 273677824 | bytes 5910528 | tf_op jit(solution)/shard_map/qd,kd->qk/dot_general | solution.py:97
  112.5 2.2 %fusion.76 = f32[8,64,128,1]{2,1,3,0:T(8,128)} fusion(f32[8,64,4,64]{1,3,2,0:T(8,128)S(1)} %get-tuple-element.68, bf16[2,8,4,64,128]{4,3,2,1,0:T(8,128)(2,1)} %bitcast.236, f32[8,64]{1,0:T(8,128)S(1)} %max.47), kind=kOutput, calls=%fused_computation.70 | convolution fusion | flops 33816576 | bytes 1312768 | tf_op jit(solution)/shard_map/wojf,wjfl->wol/dot_general | solution.py:44
  114.6 2.1 fusion.97
  116.7 3.7 %fusion.102 = (f32[512]{0:T(512)S(1)}, f32[512,2048]{0,1:T(8,128)}) fusion(bf16[2048,128]{1,0:T(8,128)(2,1)S(1)} %bitcast.256, bf16[512,512]{1,0:T(8,128)(2,1)} %param.8, pred[512,2048]{0,1:T(32,128)(4,1)S(1)} %copy-done.17, s32[512]{0:T(512)S(1)} %copy-done.37, s32[2048]{0:T(1024)S(1)} %copy-done.30), kind=kOutput, calls=%fused_computation.184 | convolution fusion | flops 273677824 | bytes 5910528 | tf_op jit(solution)/shard_map/qd,kd->qk/dot_general | solution.py:97
  120.7 2.2 fusion.74
  122.9 0.9 fusion.98
  123.8 3.7 %fusion.100 = (f32[512]{0:T(512)S(1)}, f32[512,2048]{0,1:T(8,128)}) fusion(bf16[2048,128]{1,0:T(8,128)(2,1)S(1)} %bitcast.253, bf16[512,512]{1,0:T(8,128)(2,1)} %param.8, pred[512,2048]{0,1:T(32,128)(4,1)S(1)} %copy-done.16, s32[512]{0:T(512)S(1)} %copy-done.37, s32[2048]{0:T(1024)S(1)} %copy-done.29), kind=kOutput, calls=%fused_computation.182 | convolution fusion | flops 273677824 | bytes 5910528 | tf_op jit(solution)/shard_map/qd,kd->qk/dot_general | solution.py:97
  129.0 3.0 %fusion = f32[512]{0:T(512)S(1)} fusion(f32[512,2048]{0,1:T(8,128)} %get-tuple-element.70, f32[512]{0:T(512)S(1)} %max.44), kind=kLoop, calls=%fused_computation.15 | loop fusion | flops 2096640 | bytes 4198400 | tf_op jit(solution)/shard_map/reduce_sum | solution.py:36
  134.4 0.8 copy-done.3
  136.4 0.8 fusion.61
  137.2 0.7 fusion.58
  138.0 0.8 fusion.55
  138.8 0.8 fusion.52
  140.2 56.8 %all_to_all.9 = bf16[512,8,512]{2,0,1:T(8,128)(2,1)} all-to-all(bf16[512,8,512]{2,0,1:T(8,128)(2,1)S(1)} %tile.2), channel_id=1, replica_groups=mesh['ctx'=32,'head'=8] {'head'}, dimensions={1} | all-to-all | bytes 8388608 | tf_op jit(solution)/shard_map/all_to_all | solution.py:15
  197.0 6.5 %copy.100 = bf16[512,8,512]{0,2,1:T(8,128)(2,1)} copy(bf16[512,8,512]{2,0,1:T(8,128)(2,1)} %all_to_all.9) | data formatting | bytes 8388608 | tf_op jit(solution)/shard_map/all_to_all | solution.py:15
  203.5 6.6 %convolution_convert_fusion = bf16[512,512]{1,0:T(8,128)(2,1)} fusion(bf16[512,4096]{0,1:T(8,128)(2,1)} %bitcast.226, bf16[4096,512]{1,0:T(8,128)(2,1)} %param.15), kind=kOutput, calls=%fused_computation.43 | convolution fusion | flops 2147745792 | bytes 8912896 | tf_op jit(solution)/shard_map/dot_general | solution.py:138
  (187 shorter events, 17.9 us)
Async XLA Ops:
  6.5 13.8 %copy-start.28 = (s32[4,32,1]{1,2,0:T(1,128)S(1)}, s32[4,32,1]{1,2,0:T(1,128)}, u32[]{:S(2)}) copy-start(s32[4,32,1]{1,2,0:T(1,128)} %param.13) | copy-start | bytes 1540
  6.5 13.3 %copy-start.35 = (s32[4,4]{1,0:T(4,128)S(1)}, s32[4,4]{1,0:T(4,128)}, u32[]{:S(2)}) copy-start(s32[4,4]{1,0:T(4,128)} %param.11) | copy-start | bytes 196
  6.5 14.1 %copy-start.36 = (s32[4,32]{1,0:T(4,128)S(1)}, s32[4,32]{1,0:T(4,128)}, u32[]{:S(2)}) copy-start(s32[4,32]{1,0:T(4,128)} %param.14) | copy-start | bytes 1540
  6.5 87.8 %all-gather.3.cloned.1.call-start = ((), (), s32[]{:S(2)}) async-start(), calls=%async_computation.1 | async-start | bytes 4325376 | tf_op jit(solution)/shard_map/all_gather | solution.py:76
  12.3 35.8 %collective-permute-start = (bf16[2,512,128]{2,1,0:T(8,128)(2,1)S(1)}, bf16[2,512,128]{2,1,0:T(8,128)(2,1)S(1)}, u32[]{:S(2)}, u32[]{:S(2)}) collective-permute-start(bf16[2,512,128]{2,1,0:T(8,128)(2,1)S(1)} %pad_maximum_fusion.2), channel_id=1, source_target_pairs={{0,8},{8,16},{16,24},{24,32},{32,40},{40,48},{48,56},{56,64},{64,7... | collective-permute-start | bytes 786440 | tf_op jit(solution)/shard_map/ppermute | solution.py:23
  35.8 11.5 %copy-start.22 = (bf16[512,512]{1,0:T(8,128)(2,1)S(1)}, bf16[512,512]{1,0:T(8,128)(2,1)}, u32[]{:S(2)}) copy-start(bf16[512,512]{1,0:T(8,128)(2,1)} %param.8) | copy-start | bytes 1572868
  35.8 12.2 %copy-start.14 = (bf16[512,128]{1,0:T(8,128)(2,1)S(1)}, bf16[512,128]{1,0:T(8,128)(2,1)}, u32[]{:S(2)}) copy-start(bf16[512,128]{1,0:T(8,128)(2,1)} %param.10) | copy-start | bytes 393220
  35.8 12.2 %copy-start.15 = (bf16[512,128]{1,0:T(8,128)(2,1)S(1)}, bf16[512,128]{1,0:T(8,128)(2,1)}, u32[]{:S(2)}) copy-start(bf16[512,128]{1,0:T(8,128)(2,1)} %param.9) | copy-start | bytes 393220
  46.6 3.3 %copy-start.27 = (pred[64,4,64]{0,2,1:T(8,128)(4,1)S(1)}, pred[64,4,64]{0,2,1:T(8,128)(4,1)}, u32[]{:S(2)}) copy-start(pred[64,4,64]{0,2,1:T(8,128)(4,1)} %get-tuple-element.21) | copy-start | bytes 49156
  46.6 3.3 %copy-start.41 = (pred[8,4]{1,0:T(8,128)(4,1)S(1)}, pred[8,4]{1,0:T(8,128)(4,1)}, u32[]{:S(2)}) copy-start(pred[8,4]{1,0:T(8,128)(4,1)} %get-tuple-element.49) | copy-start | bytes 100
  48.9 4.4 %copy-start.26 = (pred[64,4,64]{0,2,1:T(8,128)(4,1)S(1)}, pred[64,4,64]{0,2,1:T(8,128)(4,1)}, u32[]{:S(2)}) copy-start(pred[64,4,64]{0,2,1:T(8,128)(4,1)} %get-tuple-element.22) | copy-start | bytes 49156
  48.9 4.4 %copy-start.40 = (pred[8,4]{1,0:T(8,128)(4,1)S(1)}, pred[8,4]{1,0:T(8,128)(4,1)}, u32[]{:S(2)}) copy-start(pred[8,4]{1,0:T(8,128)(4,1)} %get-tuple-element.50) | copy-start | bytes 100
  49.0 1.0 copy-start.9
  52.1 4.0 %copy-start.23 = (bf16[512,128]{1,0:T(8,128)(2,1)S(1)}, bf16[512,128]{1,0:T(8,128)(2,1)}, u32[]{:S(2)}) copy-start(bf16[512,128]{1,0:T(8,128)(2,1)} %get-tuple-element.20) | copy-start | bytes 393220
  52.1 4.0 %copy-start.25 = (pred[64,4,64]{0,2,1:T(8,128)(4,1)S(1)}, pred[64,4,64]{0,2,1:T(8,128)(4,1)}, u32[]{:S(2)}) copy-start(pred[64,4,64]{0,2,1:T(8,128)(4,1)} %get-tuple-element.23) | copy-start | bytes 49156
  52.1 4.0 %copy-start.39 = (pred[8,4]{1,0:T(8,128)(4,1)S(1)}, pred[8,4]{1,0:T(8,128)(4,1)}, u32[]{:S(2)}) copy-start(pred[8,4]{1,0:T(8,128)(4,1)} %get-tuple-element.51) | copy-start | bytes 100
  52.2 1.0 copy-start.8
  55.0 6.1 %copy-start.24 = (pred[64,4,64]{0,2,1:T(8,128)(4,1)S(1)}, pred[64,4,64]{0,2,1:T(8,128)(4,1)}, u32[]{:S(2)}) copy-start(pred[64,4,64]{0,2,1:T(8,128)(4,1)} %get-tuple-element.24) | copy-start | bytes 49156
  55.0 6.1 %copy-start.38 = (pred[8,4]{1,0:T(8,128)(4,1)S(1)}, pred[8,4]{1,0:T(8,128)(4,1)}, u32[]{:S(2)}) copy-start(pred[8,4]{1,0:T(8,128)(4,1)} %get-tuple-element.52) | copy-start | bytes 100
  55.1 1.0 copy-start.7
  60.1 1.0 copy-start.5
  61.5 38.1 %copy-start.32 = (s32[2048]{0:T(1024)S(1)}, s32[2048]{0:T(1024)}, u32[]{:S(2)}) copy-start(s32[2048]{0:T(1024)} %add.293) | copy-start | bytes 24580
  61.5 38.1 %copy-start.37 = (s32[512]{0:T(512)S(1)}, s32[512]{0:T(512)}, u32[]{:S(2)}) copy-start(s32[512]{0:T(512)} %iota_add_fusion.4) | copy-start | bytes 6148
  94.3 5.3 %copy-start.19 = (pred[512,2048]{0,1:T(32,128)(4,1)S(1)}, pred[512,2048]{0,1:T(32,128)(4,1)}, u32[]{:S(2)}) copy-start(pred[512,2048]{0,1:T(32,128)(4,1)} %reshape.1058) | copy-start | bytes 3145732
  99.6 8.9 %copy-start.31 = (s32[2048]{0:T(1024)S(1)}, s32[2048]{0:T(1024)}, u32[]{:S(2)}) copy-start(s32[2048]{0:T(1024)} %add.307) | copy-start | bytes 24580
  103.3 5.3 %copy-start.18 = (pred[512,2048]{0,1:T(32,128)(4,1)S(1)}, pred[512,2048]{0,1:T(32,128)(4,1)}, u32[]{:S(2)}) copy-start(pred[512,2048]{0,1:T(32,128)(4,1)} %reshape.1061) | copy-start | bytes 3145732
  108.6 8.2 %copy-start.30 = (s32[2048]{0:T(1024)S(1)}, s32[2048]{0:T(1024)}, u32[]{:S(2)}) copy-start(s32[2048]{0:T(1024)} %add.314) | copy-start | bytes 24580
  112.3 4.5 %copy-start.17 = (pred[512,2048]{0,1:T(32,128)(4,1)S(1)}, pred[512,2048]{0,1:T(32,128)(4,1)}, u32[]{:S(2)}) copy-start(pred[512,2048]{0,1:T(32,128)(4,1)} %reshape.1064) | copy-start | bytes 3145732
  116.7 6.2 %copy-start.4 = (bf16[1,64,64,128]{3,2,1,0:T(8,128)(2,1)S(1)}, bf16[1,64,64,128]{3,2,1,0:T(8,128)(2,1)}, u32[]{:S(2)}) copy-start(bf16[1,64,64,128]{3,2,1,0:T(8,128)(2,1)} %get-tuple-element.8) | copy-start | bytes 3145732
  116.7 7.0 %copy-start.29 = (s32[2048]{0:T(1024)S(1)}, s32[2048]{0:T(1024)}, u32[]{:S(2)}) copy-start(s32[2048]{0:T(1024)} %add.321) | copy-start | bytes 24580
  120.5 3.2 %copy-start.16 = (pred[512,2048]{0,1:T(32,128)(4,1)S(1)}, pred[512,2048]{0,1:T(32,128)(4,1)}, u32[]{:S(2)}) copy-start(pred[512,2048]{0,1:T(32,128)(4,1)} %reshape.1067) | copy-start | bytes 3145732
  123.8 4.0 %copy-start.6 = (bf16[32,2,64,128]{3,2,0,1:T(8,128)(2,1)S(1)}, bf16[32,2,64,128]{3,2,0,1:T(8,128)(2,1)}, u32[]{:S(2)}) copy-start(bf16[32,2,64,128]{3,2,0,1:T(8,128)(2,1)} %copy-done.5) | copy-start | bytes 3145732
  123.8 4.6 %copy-start.33 = (f32[512]{0:T(512)S(1)}, f32[512]{0:T(512)}, u32[]{:S(2)}) copy-start(f32[512]{0:T(512)} %reduce_max.94) | copy-start | bytes 6148
  123.8 4.7 %copy-start.20 = (f32[8,64,128,1]{2,1,3,0:T(8,128)S(1)}, f32[8,64,128,1]{2,1,3,0:T(8,128)}, u32[]{:S(2)}) copy-start(f32[8,64,128,1]{2,1,3,0:T(8,128)} %fusion.76) | copy-start | bytes 786436
  123.8 4.8 %copy-start.34 = (f32[512]{0:T(512)S(1)}, f32[512]{0:T(512)}, u32[]{:S(2)}) copy-start(f32[512]{0:T(512)} %reduce_max.98) | copy-start | bytes 6148
  123.8 4.9 %copy-start.21 = (f32[8,64,128,1]{2,1,3,0:T(8,128)S(1)}, f32[8,64,128,1]{2,1,3,0:T(8,128)}, u32[]{:S(2)}) copy-start(f32[8,64,128,1]{2,1,3,0:T(8,128)} %fusion.74) | copy-start | bytes 786436
  128.9 6.9 %copy-start.10 = (bf16[32,1,1,64,128]{4,3,2,0,1:T(8,128)(2,1)S(1)}, bf16[32,1,1,64,128]{4,3,2,0,1:T(8,128)(2,1)}, u32[]{:S(2)}) copy-start(bf16[32,1,1,64,128]{4,3,2,0,1:T(8,128)(2,1)} %get-tuple-element.9) | copy-start | bytes 1572868
  129.0 3.5 %copy-start.1 = (f32[512,2048]{0,1:T(8,128)S(1)}, f32[512,2048]{0,1:T(8,128)}, u32[]{:S(2)}) copy-start(f32[512,2048]{0,1:T(8,128)} %get-tuple-element.66) | copy-start | bytes 12582916
  129.0 4.7 %copy-start.2 = (f32[512,2048]{0,1:T(8,128)S(1)}, f32[512,2048]{0,1:T(8,128)}, u32[]{:S(2)}) copy-start(f32[512,2048]{0,1:T(8,128)} %get-tuple-element.62) | copy-start | bytes 12582916
  132.5 2.7 %copy-start.3 = (f32[512,2048]{0,1:T(8,128)S(1)}, f32[512,2048]{0,1:T(8,128)}, u32[]{:S(2)}) copy-start(f32[512,2048]{0,1:T(8,128)} %get-tuple-element.58) | copy-start | bytes 12582916
  133.8 2.7 %copy-start = (f32[512,2048]{0,1:T(8,128)S(1)}, f32[512,2048]{0,1:T(8,128)}, u32[]{:S(2)}) copy-start(f32[512,2048]{0,1:T(8,128)} %get-tuple-element.70) | copy-start | bytes 12582916
  135.2 2.0 copy-start.11
  136.4 1.5 copy-start.12
  137.2 1.5 copy-start.13
Sparse Core Ops, SparseCore 0:
  11.4 82.8 all-gather.2
